TPU v7x, 512 devices: a whole 4x4x16 slice. The times are simulated.
512 devices in a mesh: alt: 8 (over x, y_hi), strip: 64 (over z, y_lo, core).
Axes of the slice: x: 4, y: 4 (y_hi: 2, y_lo: 2; y = y_hi * 2 + y_lo), z: 16, core: 2. Of those that a mesh axis runs over, the one named last changes fastest.
Arguments:
- screens: bfloat16 [16, 512, 512], P('alt', 'strip'), may hold values from -2.390625 to 2.390625
- row_offset: int32 [2, 16, 2], replicated, may hold values from 0 to 341, as said below
- col_offset: int32 [2, 16, 2], replicated, may hold values from 0 to 341, as said below
- layer_bin: int32 [16], replicated, may hold values from 0 to 15
- illumination: float32 [16, 12800], P(None, ('alt', 'strip')), may hold values from 0.3 to 1
- reconstructor: bfloat16 [2, 12800, 6000], P(None, ('alt', 'strip')), may hold values from -0.0390625 to 0.0390625
- sat_code: int32 [6000], replicated, may hold values from 1 to 16
Outputs:
- slopes: float32 [2, 2, 12800], P(None, None, ('alt', 'strip'))
- commands: float32 [2, 6000], replicated
Inputs may be any that keep to these rules, and one draw needn't show every extreme that they name: Every footprint lies inside the screen: row_offset[f, l, g] + (319) shrink_l <= 511. Every footprint lies inside the screen: col_offset[f, l, g] + (319) shrink_l <= 511.
All inputs are finite; a program needn't handle non-finite values.
Results may differ from a plain program's by a relative error of at most 0.0028.
Values sent between devices are 32-bit elements; how exact they have to be, the bound alone decides.
No kernel may reach another device: no remote copies, remote signals or barrier semaphores. Data moves between devices by JAX's collectives and lax.ppermute only.
A program may use at most 64 MiB of HBM per device.

v0:
```python
import math
import jax
import jax.numpy as jnp
from jax import lax
from jax.sharding import PartitionSpec as P

LENSLETS = 80
PIXELS = 4
GUIDE_STARS = 2
FRAMES = 2
ACTUATORS = 6000
PUPIL_PIX = 320
WINDOW = 384
SUBAPS_ALL = 12800
highest = lax.Precision.HIGHEST
loop_gain = 0.5
code_step = 0.125
bin_step = 0.03125


def bilinear(offsets):
    return jnp.maximum(0.0, 1.0 - jnp.abs(offsets))


def dft_tables():
    padded = 2 * PIXELS
    freq_index = jnp.arange(padded * padded, dtype=jnp.int32)
    freq_row = freq_index // padded
    freq_col = freq_index % padded
    pix_index = jnp.arange(PIXELS * PIXELS, dtype=jnp.int32)
    pix_row = pix_index // PIXELS
    pix_col = pix_index % PIXELS
    turn_count = (
        freq_row[:, None] * pix_row[None, :] + freq_col[:, None] * pix_col[None, :]
    ) % padded
    angles = turn_count.astype(jnp.float32) * (2.0 * math.pi / padded)
    coord_row = ((freq_row + PIXELS) % padded - PIXELS).astype(jnp.float32)
    coord_col = ((freq_col + PIXELS) % padded - PIXELS).astype(jnp.float32)
    return (jnp.cos(angles), jnp.sin(angles), coord_row, coord_col)


def centroids(pupil_phase, illumination, tables):
    cosine, sine_table, coord_row, coord_col = tables
    field_re = illumination * jnp.cos(pupil_phase)
    field_im = illumination * jnp.sin(pupil_phase)
    real_part = jnp.dot(cosine, field_re, precision=highest) + jnp.dot(
        sine_table, field_im, precision=highest
    )
    imag_part = jnp.dot(cosine, field_im, precision=highest) - jnp.dot(
        sine_table, field_re, precision=highest
    )
    intensity = real_part * real_part + imag_part * imag_part
    flux_sum = jnp.sum(intensity, axis=0)
    slope_row = jnp.sum(intensity * coord_row[:, None], axis=0) / flux_sum
    slope_col = jnp.sum(intensity * coord_col[:, None], axis=0) / flux_sum
    return jnp.stack([slope_row, slope_col])


def shards(screens, row_offset, col_offset, layer_bin, illumination, reconstructor, sat_code):
    layer_dev = screens.shape[0]
    rows_here = screens.shape[1]
    count_here = illumination.shape[1]
    group_pos = lax.axis_index("alt")
    strip_pos = lax.axis_index("strip")
    row_global = strip_pos * rows_here + jnp.arange(rows_here, dtype=jnp.int32)
    pupil_idx = jnp.arange(PUPIL_PIX, dtype=jnp.float32)
    window_idx = jnp.arange(WINDOW, dtype=jnp.float32)
    widened_layers = [
        jnp.pad(screens[layer_no], ((0, 0), (0, WINDOW))) for layer_no in range(layer_dev)
    ]
    frame_terms = []
    for frame_no in range(FRAMES):
        running = jnp.zeros((PIXELS, PIXELS, GUIDE_STARS, LENSLETS, LENSLETS), jnp.float32)
        for layer_no in range(layer_dev):
            layer_pos = group_pos * layer_dev + layer_no
            tops = lax.dynamic_index_in_dim(row_offset[frame_no], layer_pos, 0, keepdims=False)
            lefts = lax.dynamic_index_in_dim(col_offset[frame_no], layer_pos, 0, keepdims=False)
            bin_value = lax.dynamic_index_in_dim(layer_bin, layer_pos, 0, keepdims=False)
            shrink = 1.0 - bin_value.astype(jnp.float32) * bin_step
            col_weights = bilinear(window_idx[None, :] - pupil_idx[:, None] * shrink)
            widened = widened_layers[layer_no]

            def cut_columns(left_col):
                return lax.dynamic_slice_in_dim(widened, left_col, WINDOW, 1)

            strips = jax.vmap(cut_columns)(lefts).astype(jnp.float32)
            across = jnp.einsum("drc,jc->drj", strips, col_weights, precision=highest)
            offsets = (row_global[None, :] - tops[:, None]).astype(jnp.float32)
            row_weights = bilinear(offsets[:, None, :] - pupil_idx[None, :, None] * shrink)
            running = running + jnp.einsum(
                "dapr,drbq->pqdab",
                row_weights.reshape(GUIDE_STARS, LENSLETS, PIXELS, rows_here),
                across.reshape(GUIDE_STARS, rows_here, LENSLETS, PIXELS),
                precision=highest,
            )
        frame_terms.append(running.reshape(PIXELS * PIXELS, SUBAPS_ALL))
    phase_terms = jnp.concatenate(frame_terms, axis=0)
    owned = lax.psum_scatter(phase_terms, ("alt", "strip"), scatter_dimension=1, tiled=True)
    pupil_phase = owned.reshape(FRAMES, PIXELS * PIXELS, count_here)
    tables = dft_tables()
    slopes = jnp.stack(
        [centroids(pupil_phase[frame_no], illumination, tables) for frame_no in range(FRAMES)]
    )
    rounded = slopes.astype(jnp.bfloat16).reshape(FRAMES, 2 * count_here)
    partial_value = jnp.dot(
        rounded,
        reconstructor.reshape(2 * count_here, ACTUATORS),
        preferred_element_type=jnp.float32,
    )
    updates = lax.psum(partial_value, ("alt", "strip"))
    limits = sat_code.astype(jnp.float32) * code_step
    first_cmd = jnp.clip(loop_gain * updates[0], -limits, limits)
    second_cmd = jnp.clip(first_cmd + loop_gain * updates[1], -limits, limits)
    return (slopes, jnp.stack([first_cmd, second_cmd]))


def solution(mesh):
    placed = (
        P("alt", "strip", None),
        P(),
        P(),
        P(),
        P(None, ("alt", "strip")),
        P(None, ("alt", "strip"), None),
        P(),
    )
    return jax.shard_map(
        shards,
        mesh=mesh,
        in_specs=placed,
        out_specs=(P(None, None, ("alt", "strip")), P()),
        check_vma=False,
    )
```

profile of v0, /device:TPU:1, one launch (start us, length us, event | category | flops | bytes accessed | tf_op | source)
XLA Modules:
  0.0 635.3 jit_solution(2373824298019678638)
XLA Ops:
  7.2 1.4 fusion.161
  10.0 0.7 fusion.159
  10.8 0.7 fusion.160
  11.8 0.7 slice_bitcast_fusion
  12.6 2.7 while.4
  13.2 0.7 bitcast_dynamic-update-slice_fusion.8
  14.6 0.7 bitcast_dynamic-update-slice_fusion.8
  15.5 2.5 while.5
  19.2 1.2 fusion.21
  20.5 1.2 fusion.1
  22.1 1.7 reshape.445
  24.2 2.7 while.6
  24.8 0.7 bitcast_dynamic-update-slice_fusion.10
  26.2 0.7 bitcast_dynamic-update-slice_fusion.10
  27.6 2.6 while.7
  28.2 0.7 bitcast_dynamic-update-slice_fusion.11
  29.5 0.7 bitcast_dynamic-update-slice_fusion.11
  30.8 1.2 fusion.18
  32.0 1.2 fusion
  33.7 1.7 reshape.448
  35.4 2.5 pad_maximum_fusion
  38.0 477.4 %all-reduce.9.cloned.1.call-done = f32[32,12800]{1,0:T(8,128)} async-done(((f32[32,12800]{1,0:T(8,128)}), f32[32,12800]{1,0:T(8,128)}) %all-reduce.9.cloned.1.call-update) | async-done | bytes 1638416
  515.4 1.1 fusion.84
  516.5 1.1 fusion.82
  517.6 1.1 fusion.80
  518.7 1.1 fusion.78
  519.9 1.1 fusion.4
  521.0 1.1 fusion.7
  522.2 1.1 fusion.6
  523.3 1.3 multiply_reduce_fusion.1
  525.0 102.0 %psum.7 = f32[2,6000]{1,0:T(2,128)S(1)} all-reduce(f32[2,6000]{1,0:T(2,128)S(1)} %convolution_bitcast_fusion), channel_id=1, replica_groups=mesh['alt'=8,'strip'=64] {'alt','strip'}, use_global_device_ids=true, to_apply=%region_7.8 | all-reduce | flops 12000 | bytes 96000 | tf_op jit(solution)/shard_map/psum | solution.py:110
  627.8 0.7 pad_maximum_fusion.1
  (73 shorter events, 11.6 us)
Async XLA Ops:
  7.2 517.5 %copy-start = (bf16[2,25,6000]{2,0,1:T(2,128)(2,1)S(1)}, bf16[2,25,6000]{2,0,1:T(2,128)(2,1)}, u32[]{:S(2)}) copy-start(bf16[2,25,6000]{2,0,1:T(2,128)(2,1)} %param.12) | copy-start | bytes 1800004
  7.2 508.2 %all-reduce.9.cloned.1.call-start = ((), (), s32[]{:S(2)}) async-start(), calls=%async_computation | async-start | bytes 3276800
  33.6 1.7 copy-start.1
  37.9 477.5 %copy-start.3 = (f32[16,25]{1,0:T(8,128)S(1)}, f32[16,25]{1,0:T(8,128)}, u32[]{:S(2)}) copy-start(f32[16,25]{1,0:T(8,128)} %param.11) | copy-start | bytes 4804
  37.9 589.2 %copy-start.2 = (s32[6000]{0:T(1024)S(1)}, s32[6000]{0:T(1024)}, u32[]{:S(2)}) copy-start(s32[6000]{0:T(1024)} %param.13) | copy-start | bytes 72004
Sparse Core Ops, SparseCore 0:
  38.0 477.3 all-reduce.8
where the time goes:
time: 636 us; the launch traced here: 635 us
  waiting for transfers between devices  477 us (75%)
  blocking collectives  102 us (16%)
  local copies, waits for them, and re-layouts  20.2 us (3%)
  matrix products  16.4 us (3%)
  between operations  15.7 us (2%)
    unnamed x2, waiting for transfers between devices  477 us
    psum x1, blocking collectives, shards(): updates = lax.psum(partial_value, ('alt', 'strip'))  102 us
  transfers between devices with their start and end apart: 1, of which 1 were waited for; matrix products, arithmetic and copies ran while one was open for 0% of the time, Pallas kernels for 0%

commit v1 on v0

--- a/solution.py
+++ b/solution.py
@@ -107,7 +107,7 @@
         reconstructor.reshape(2 * count_here, ACTUATORS),
         preferred_element_type=jnp.float32,
     )
-    updates = lax.psum(partial_value, ("alt", "strip"))
+    updates = jnp.sum(lax.all_gather(partial_value, ("alt", "strip")), axis=0)
     limits = sat_code.astype(jnp.float32) * code_step
     first_cmd = jnp.clip(loop_gain * updates[0], -limits, limits)
     second_cmd = jnp.clip(first_cmd + loop_gain * updates[1], -limits, limits)

time: 636 us -> 1390 us (2.19)
  waiting for transfers between devices: 477 us -> 1320 us
  blocking collectives: 102 us -> 0 us
    all_gather x0 -> x1, waiting for transfers between devices: none -> 838 us  [shards(): updates = jnp.sum(lax.all_gather(partial_value, ('alt', 'strip')), axis=0)]
    psum x1 -> x0, blocking collectives: 102 us -> none  [shards(): updates = lax.psum(partial_value, ('alt', 'strip'))]
    unnamed x2 -> x3, waiting for transfers between devices: 477 us -> 477 us
  transfers between devices with their start and end apart: 1 -> 2, of which waited for: 1 -> 2; matrix products, arithmetic and copies ran while one was open for 0% -> 0% of each run, Pallas kernels for 0% -> 0%
where the time goes in v1:
time: 1390 us; the launch traced here: 1380 us
  waiting for transfers between devices  1320 us (95%)
  local copies, waits for them, and re-layouts  20.3 us (1%)
  matrix products  17.8 us (1%)
  between operations  15.7 us (1%)
    all_gather x1, waiting for transfers between devices, shards(): updates = jnp.sum(lax.all_gather(partial_value, ('alt', 'strip')), axis=0)  838 us
    unnamed x3, waiting for transfers between devices  477 us
  transfers between devices with their start and end apart: 2, of which 2 were waited for; matrix products, arithmetic and copies ran while one was open for 0% of the time, Pallas kernels for 0%

profile of v1, /device:TPU:1, one launch (start us, length us, event | category | flops | bytes accessed | tf_op | source)
XLA Modules:
  0.0 1383.1 jit_solution(18230725256749544686)
XLA Ops:
  7.2 1.4 fusion.161
  12.5 0.7 slice_bitcast_fusion
  13.3 2.8 while.7
  13.9 0.7 bitcast_dynamic-update-slice_fusion.11
  15.3 0.7 bitcast_dynamic-update-slice_fusion.11
  16.0 2.7 while.5
  16.7 0.7 bitcast_dynamic-update-slice_fusion.9
  18.0 0.7 bitcast_dynamic-update-slice_fusion.9
  18.7 2.5 while.6
  21.2 2.6 while.4
  21.8 0.7 bitcast_dynamic-update-slice_fusion.8
  23.1 0.7 bitcast_dynamic-update-slice_fusion.8
  23.9 1.2 fusion.15
  27.5 1.2 fusion.18
  28.7 1.2 fusion
  30.4 1.7 reshape.448
  32.1 1.2 fusion.21
  33.4 1.2 fusion.1
  35.0 1.7 reshape.445
  36.8 2.5 pad_maximum_fusion
  39.6 477.1 %all-reduce.9.cloned.1.call-done = f32[32,12800]{1,0:T(8,128)} async-done(((f32[32,12800]{1,0:T(8,128)}), f32[32,12800]{1,0:T(8,128)}) %all-reduce.9.cloned.1.call-update) | async-done | bytes 1638416
  516.7 1.1 fusion.82
  517.8 1.1 fusion.84
  518.9 1.1 fusion.78
  520.1 1.1 fusion.80
  521.2 1.1 fusion.7
  522.3 1.1 fusion.4
  523.5 1.1 fusion.6
  524.6 1.3 multiply_reduce_fusion.1
  526.0 0.9 convolution_bitcast_fusion
  527.6 838.5 %all-gather.4.cloned.1.call-done = f32[512,2,6000]{2,1,0:T(2,128)} async-done(((f32[1,2,6000]{2,1,0:T(2,128)}), f32[512,2,6000]{2,1,0:T(2,128)}) %all-gather.4.cloned.1.call-update) | async-done | bytes 24576016 | tf_op jit(solution)/shard_map/all_gather | solution.py:110
  1366.1 9.3 reduce_sum.69
  (86 shorter events, 13.8 us)
Async XLA Ops:
  7.2 518.9 %copy-start = (bf16[2,25,6000]{2,0,1:T(2,128)(2,1)S(1)}, bf16[2,25,6000]{2,0,1:T(2,128)(2,1)}, u32[]{:S(2)}) copy-start(bf16[2,25,6000]{2,0,1:T(2,128)(2,1)} %param.12) | copy-start | bytes 1800004
  7.2 509.5 %all-reduce.9.cloned.1.call-start = ((), (), s32[]{:S(2)}) async-start(), calls=%async_computation.1 | async-start | bytes 3276800
  10.0 17.6 %copy-start.4 = (f32[80,4]{0,1:T(4,128)}, f32[80,4]{0,1:T(4,128)S(1)}, u32[]{:S(2)}) copy-start(f32[80,4]{0,1:T(4,128)S(1)} %fusion.91) | copy-start | bytes 3844
  30.4 1.7 copy-start.2
  30.4 1.7 copy-start.5
  30.4 1.7 copy-start.7
  32.1 1.2 copy-start.6
  35.0 1.7 copy-start.1
  39.3 477.4 %copy-start.8 = (f32[16,25]{1,0:T(8,128)S(1)}, f32[16,25]{1,0:T(8,128)}, u32[]{:S(2)}) copy-start(f32[16,25]{1,0:T(8,128)} %param.11) | copy-start | bytes 4804
  39.3 1326.7 %all-gather.4.cloned.1.call-start = ((), (), s32[]{:S(2)}) async-start(), calls=%async_computation | async-start | bytes 24689664 | tf_op jit(solution)/shard_map/all_gather | solution.py:110
  527.6 847.9 %copy-start.3 = (s32[6000]{0:T(1024)S(1)}, s32[6000]{0:T(1024)}, u32[]{:S(2)}) copy-start(s32[6000]{0:T(1024)} %param.13) | copy-start | bytes 72004
Sparse Core Ops, SparseCore 0:
  39.5 477.2 all-reduce.8
  527.1 838.9 all-gather.3

commit v2 on v0

--- a/solution.py
+++ b/solution.py
@@ -107,7 +107,7 @@
         reconstructor.reshape(2 * count_here, ACTUATORS),
         preferred_element_type=jnp.float32,
     )
-    updates = lax.psum(partial_value, ("alt", "strip"))
+    updates = lax.psum(lax.psum(partial_value, "alt"), "strip")
     limits = sat_code.astype(jnp.float32) * code_step
     first_cmd = jnp.clip(loop_gain * updates[0], -limits, limits)
     second_cmd = jnp.clip(first_cmd + loop_gain * updates[1], -limits, limits)

time: 636 us -> 779 us (1.22)
  blocking collectives: 102 us -> 244 us
    psum x1 -> x2, blocking collectives: 102 us -> 244 us  [shards(): updates = lax.psum(lax.psum(partial_value, 'alt'), 'strip')]
where the time goes in v2:
time: 779 us; the launch traced here: 778 us
  waiting for transfers between devices  477 us (61%)
  blocking collectives  244 us (31%)
  local copies, waits for them, and re-layouts  20.2 us (3%)
  matrix products  16.4 us (2%)
  between operations  15.7 us (2%)
    unnamed x2, waiting for transfers between devices  477 us
    psum x2, blocking collectives, shards(): updates = lax.psum(lax.psum(partial_value, 'alt'), 'strip')  244 us
  transfers between devices with their start and end apart: 1, of which 1 were waited for; matrix products, arithmetic and copies ran while one was open for 0% of the time, Pallas kernels for 0%

profile of v2, /device:TPU:1, one launch (start us, length us, event | category | flops | bytes accessed | tf_op | source)
XLA Modules:
  0.0 777.6 jit_solution(12831771296193518723)
XLA Ops:
  7.2 1.4 fusion.161
  10.0 0.7 fusion.159
  10.8 0.7 fusion.160
  11.8 0.7 slice_bitcast_fusion
  12.6 2.7 while.4
  13.2 0.7 bitcast_dynamic-update-slice_fusion.8
  14.6 0.7 bitcast_dynamic-update-slice_fusion.8
  15.5 2.5 while.5
  19.2 1.2 fusion.21
  20.5 1.2 fusion.1
  22.1 1.7 reshape.445
  24.2 2.7 while.6
  24.8 0.7 bitcast_dynamic-update-slice_fusion.10
  26.2 0.7 bitcast_dynamic-update-slice_fusion.10
  27.6 2.6 while.7
  28.2 0.7 bitcast_dynamic-update-slice_fusion.11
  29.5 0.7 bitcast_dynamic-update-slice_fusion.11
  30.8 1.2 fusion.18
  32.0 1.2 fusion
  33.7 1.7 reshape.448
  35.4 2.5 pad_maximum_fusion
  38.0 477.4 %all-reduce.9.cloned.1.call-done = f32[32,12800]{1,0:T(8,128)} async-done(((f32[32,12800]{1,0:T(8,128)}), f32[32,12800]{1,0:T(8,128)}) %all-reduce.9.cloned.1.call-update) | async-done | bytes 1638416
  515.4 1.1 fusion.84
  516.5 1.1 fusion.82
  517.6 1.1 fusion.80
  518.7 1.1 fusion.78
  519.9 1.1 fusion.4
  521.0 1.1 fusion.7
  522.2 1.1 fusion.6
  523.3 1.3 multiply_reduce_fusion.1
  525.0 34.9 %psum.14 = f32[2,6000]{1,0:T(2,128)S(1)} all-reduce(f32[2,6000]{1,0:T(2,128)S(1)} %convolution_bitcast_fusion), channel_id=1, replica_groups=mesh['alt'=8,'strip'=64] {'alt'}, use_global_device_ids=true, to_apply=%region_7.8 | all-reduce | flops 12000 | bytes 96000 | tf_op jit(solution)/shard_map/psum | solution.py:110
  559.9 209.5 %psum.15 = f32[2,6000]{1,0:T(2,128)S(1)} all-reduce(f32[2,6000]{1,0:T(2,128)S(1)} %psum.14), channel_id=1, replica_groups=mesh['alt'=8,'strip'=64] {'strip'}, use_global_device_ids=true, to_apply=%region_8.9 | all-reduce | flops 12000 | bytes 96000 | tf_op jit(solution)/shard_map/psum | solution.py:110
  (74 shorter events, 12.3 us)
Async XLA Ops:
  7.2 517.5 %copy-start = (bf16[2,25,6000]{2,0,1:T(2,128)(2,1)S(1)}, bf16[2,25,6000]{2,0,1:T(2,128)(2,1)}, u32[]{:S(2)}) copy-start(bf16[2,25,6000]{2,0,1:T(2,128)(2,1)} %param.12) | copy-start | bytes 1800004
  7.2 508.2 %all-reduce.9.cloned.1.call-start = ((), (), s32[]{:S(2)}) async-start(), calls=%async_computation | async-start | bytes 3276800
  33.6 1.7 copy-start.1
  37.9 477.5 %copy-start.3 = (f32[16,25]{1,0:T(8,128)S(1)}, f32[16,25]{1,0:T(8,128)}, u32[]{:S(2)}) copy-start(f32[16,25]{1,0:T(8,128)} %param.11) | copy-start | bytes 4804
  37.9 731.6 %copy-start.2 = (s32[6000]{0:T(1024)S(1)}, s32[6000]{0:T(1024)}, u32[]{:S(2)}) copy-start(s32[6000]{0:T(1024)} %param.13) | copy-start | bytes 72004
Sparse Core Ops, SparseCore 0:
  38.0 477.3 all-reduce.8
